TPU v7x, 1024 devices: a whole 8x8x8 slice. The times are simulated.
1024 devices in a mesh: row: 8 (over x), col: 8 (over z), layer: 16 (over y, core).
Axes of the slice: x: 8, y: 8, z: 8, core: 2. Of those that a mesh axis runs over, the one named last changes fastest.
Arguments:
- a_blocks: bfloat16 [2048, 128, 128], P(('row', 'col', 'layer')), may hold values from -0.25 to 0.25
- a_slot: int32 [2048], P(('row', 'col', 'layer')), may hold values from 0 to 63, as said below
- b_blocks: bfloat16 [1024, 128, 128], P(('row', 'col', 'layer')), may hold values from -6 to 6
- b_slot: int32 [1024], P(('row', 'col', 'layer')), may hold values from 0 to 31, as said below
- c_mask: int32 [128, 64], P('row', 'col'), may hold values from 0 to 1, as said below
Outputs:
- product: float32 [16384, 8192], P(('row', 'layer'), 'col')
Inputs may be any that keep to these rules, and one draw needn't show every extreme that they name: `a_slot`: within each row panel r and inner slice l the 16 slots of A are distinct. `b_slot`: within each column panel c and inner slice l the 8 slots of B are distinct. `c_mask`: every block row has exactly 4 ones in each column panel of 8 block columns.
All inputs are finite; a program needn't handle non-finite values.
Results may differ from a plain program's by a relative error of at most 0.0003.
Values may be sent and summed in bfloat16 or wider, within the bound.
A program may use at most 32 MiB of HBM per device.

v0:
```python
import jax
import jax.numpy as jnp
from jax import lax
from jax.sharding import PartitionSpec as P

MBP = 16
KBL = 4
NBP = 8


def slot_table(slots, count):
    return (slots[:, None] == jnp.arange(count, dtype=jnp.int32)[None, :]).astype(jnp.bfloat16)


def add_blocks(piece):
    table, blocks = piece
    flat = blocks.reshape(blocks.shape[0], blocks.shape[1] * blocks.shape[2])
    return jnp.dot(table.T, flat, preferred_element_type=jnp.float32)


def on_device(a_blocks, a_slot, b_blocks, b_slot, c_mask):
    width = a_blocks.shape[-1]
    a_table = slot_table(a_slot, MBP * KBL)
    b_table = slot_table(b_slot, KBL * NBP)
    a_dense = add_blocks(
        (
            lax.all_gather(a_table, "col", axis=0, tiled=True),
            lax.all_gather(a_blocks, "col", axis=0, tiled=True),
        )
    )
    b_dense = add_blocks(
        (
            lax.all_gather(b_table, "row", axis=0, tiled=True),
            lax.all_gather(b_blocks, "row", axis=0, tiled=True),
        )
    )
    a_matrix = (
        a_dense.astype(jnp.bfloat16)
        .reshape(MBP, KBL, width, width)
        .transpose(0, 2, 1, 3)
        .reshape(MBP * width, KBL * width)
    )
    b_matrix = (
        b_dense.astype(jnp.bfloat16)
        .reshape(KBL, NBP, width, width)
        .transpose(0, 2, 1, 3)
        .reshape(KBL * width, NBP * width)
    )
    partial_value = jnp.dot(a_matrix, b_matrix, preferred_element_type=jnp.float32)
    rows_dev = MBP * width // lax.axis_size("layer")
    first_row = lax.axis_index("layer") * rows_dev
    own_block = (first_row + jnp.arange(rows_dev, dtype=jnp.int32)) // width
    row_pick = (own_block[:, None] == jnp.arange(MBP, dtype=jnp.int32)[None, :]).astype(jnp.float32)
    mask_float = c_mask.astype(jnp.float32)
    summed = lax.psum_scatter(partial_value, "layer", scatter_dimension=0, tiled=True)
    row_mask = jnp.dot(row_pick, mask_float, precision=lax.Precision.HIGHEST)
    return (summed.reshape(rows_dev, NBP, width) * row_mask[:, :, None]).reshape(
        rows_dev, NBP * width
    )


def solution(mesh):
    in_specs = (
        P(("row", "col", "layer"), None, None),
        P(("row", "col", "layer")),
        P(("row", "col", "layer"), None, None),
        P(("row", "col", "layer")),
        P("row", "col"),
    )
    out_specs = P(("row", "layer"), "col")
    return jax.shard_map(
        on_device, mesh=mesh, in_specs=in_specs, out_specs=out_specs, check_vma=False
    )
```

profile of v0, /device:TPU:1, one launch (start us, length us, event | category | flops | bytes accessed | tf_op | source)
XLA Modules:
  0.0 194.6 jit_solution(13125090303734541991)
XLA Ops:
  6.5 0.0 reduce-scatter.2.cloned.1.call-start
  6.5 33.0 %all_gather.13 = bf16[16,128,128]{2,1,0:T(8,128)(2,1)S(1)} all-gather(bf16[2,128,128]{2,1,0:T(8,128)(2,1)} %param.5), channel_id=1, replica_groups=mesh['row'=8,'col'=8,'layer'=16] {'col'}, dimensions={0}, use_global_device_ids=true | all-gather | bytes 589824 | tf_op jit(solution)/shard_map/all_gather | solution.py:28
  39.6 0.7 fusion.15
  40.3 12.2 %all-gather = bf16[8,2,64]{2,1,0:T(2,128)(2,1)S(1)} all-gather(bf16[1,2,64]{2,1,0:T(2,128)(2,1)S(1)} %fusion.15), channel_id=1, replica_groups=mesh['row'=8,'col'=8,'layer'=16] {'col'}, dimensions={0}, use_global_device_ids=true | all-gather | bytes 2304 | tf_op jit(solution)/shard_map/all_gather | solution.py:27
  52.5 0.7 fusion.3
  53.3 0.6 copy.14
  53.8 0.0 copy-start
  53.8 2.9 %copy.9 = bf16[16,4,128,128]{2,0,3,1:T(8,128)(2,1)} copy(bf16[16,4,128,128]{3,2,1,0:T(8,128)(2,1)S(1)} %bitcast.42) | data formatting | bytes 4194304 | tf_op jit(solution)/shard_map/reshape | solution.py:39
  56.8 0.0 copy-done
  56.8 20.3 %all_gather.15 = bf16[8,128,128]{2,1,0:T(8,128)(2,1)S(1)} all-gather(bf16[1,128,128]{2,1,0:T(8,128)(2,1)S(1)} %copy-done), channel_id=1, replica_groups=mesh['row'=8,'col'=8,'layer'=16] {'row'}, dimensions={0}, use_global_device_ids=true | all-gather | bytes 294912 | tf_op jit(solution)/shard_map/all_gather | solution.py:34
  77.7 11.1 %all-gather.1 = bf16[8,1,32]{2,1,0:T(2,128)(2,1)S(1)} all-gather(bf16[1,1,32]{2,1,0:T(2,128)(2,1)S(1)} %fusion.16), channel_id=1, replica_groups=mesh['row'=8,'col'=8,'layer'=16] {'row'}, dimensions={0}, use_global_device_ids=true | all-gather | bytes 576 | tf_op jit(solution)/shard_map/all_gather | solution.py:33
  88.8 0.5 convolution_convert_fusion.1
  89.3 7.2 %fusion = f32[2048,1024]{1,0:T(8,128)} fusion(bf16[64,8,16,128]{3,2,1,0:T(8,128)(2,1)} %bitcast.45, bf16[64,8,8,128]{3,2,1,0:T(8,128)(2,1)S(1)} %bitcast.46), kind=kOutput, calls=%fused_computation.2 | convolution fusion | flops 2147483648 | bytes 11534336 | tf_op jit(solution)/shard_map/dot_general | solution.py:49
  96.5 0.0 copy-start.1
  96.5 0.0 reduce-scatter.2.cloned.1.call-update
  96.6 0.6 copy-done.1
  97.2 0.2 fusion.10
  97.5 88.2 %reduce-scatter.2.cloned.1.call-done = f32[128,1024]{1,0:T(8,128)} async-done(((f32[2048,1024]{1,0:T(8,128)}), f32[128,1024]{1,0:T(8,128)}) %reduce-scatter.2.cloned.1.call-update) | async-done | bytes 524304 | tf_op jit(solution)/shard_map/reduce_scatter | solution.py:55
  185.6 0.2 mul.15
  185.8 2.0 %bitcast_multiply_fusion = f32[128,1024]{1,0:T(8,128)} fusion(f32[128,1024]{1,0:T(8,128)} %reduce-scatter.2.cloned.1.call-done, f32[16,8,8,128]{3,2,1,0:T(8,128)S(1)} %bitcast.44), kind=kLoop, calls=%fused_computation.8 | loop fusion | flops 131072 | bytes 1572864 | tf_op jit(solution)/shard_map/mul | solution.py:57
  (2 shorter events, 0.0 us)
Async XLA Ops:
  6.5 179.1 %reduce-scatter.2.cloned.1.call-start = ((), (), s32[]{:S(2)}) async-start(), calls=%async_computation.1 | async-start | bytes 8912896 | tf_op jit(solution)/shard_map/reduce_scatter | solution.py:55
  53.8 2.9 %copy-start = (bf16[1,128,128]{2,1,0:T(8,128)(2,1)S(1)}, bf16[1,128,128]{2,1,0:T(8,128)(2,1)}, u32[]{:S(2)}) copy-start(bf16[1,128,128]{2,1,0:T(8,128)(2,1)} %param.7) | copy-start | bytes 98308
  96.5 0.7 copy-start.1
Sparse Core Ops, SparseCore 0:
  96.7 88.8 reduce-scatter.1
where the time goes:
time: 195 us
  waiting for transfers between devices  88.2 us (45%)
  blocking collectives  76.6 us (39%)
  between operations  14.1 us (7%)
  matrix products  8.67 us (4%)
  local copies, waits for them, and re-layouts  4.34 us (2%)
  other arithmetic  2.71 us (1%)
    reduce_scatter x1, waiting for transfers between devices, on_device(): lax.psum_scatter(partial_value, 'layer', scatter_dimension=0, tiled=True)  88.2 us
    all_gather x1, blocking collectives, on_device(): lax.all_gather(a_blocks, 'col', axis=0, tiled=True)  33 us
    all_gather x1, blocking collectives, on_device(): lax.all_gather(b_blocks, 'row', axis=0, tiled=True)  20.3 us
    all_gather x1, blocking collectives, on_device(): lax.all_gather(a_table, 'col', axis=0, tiled=True)  12.2 us
    all_gather x1, blocking collectives, on_device(): lax.all_gather(b_table, 'row', axis=0, tiled=True)  11.1 us
    dot_general x1, matrix products, on_device(): jnp.dot(a_matrix, b_matrix, preferred_element_type=jnp.float32)  7.23 us
  transfers between devices with their start and end apart: 1, of which 1 were waited for; matrix products, arithmetic and copies ran while one was open for 0% of the time, Pallas kernels for 0%

commit v1 on v0

v1 whole, which is shorter than its diff:
```python
import functools

import jax
import jax.numpy as jnp
from jax import lax
from jax.experimental import pallas as pl
from jax.experimental.pallas import tpu as pltpu
from jax.sharding import PartitionSpec as P

MESH = pl.DeviceIdType.MESH
BS = 128
ROWS = 16
INNER = 4
COLS = 8
KEPT = 4
RING = 8
TOP = 32760.0
TINY = 1e-30


def wait_bytes(ref, sem):
    pltpu.make_async_copy(ref, ref, sem).wait()


def kernel(
    a_in, a_slot, b_in, b_slot, mask, out,
    a_buf, b_buf, a_tab, b_tab, sum_tx, sum_rx, tab_v, tab_s, sel, tx, tx_scale, rx, rx_scale, comp,
    own_sem, a_recv, b_recv, sib_recv, tab_recv, tab_local, a_send, b_send, tab_send, rs_recv, rs_send,
):
    x, z, layer = lax.axis_index("row"), lax.axis_index("col"), lax.axis_index("layer")
    y, core = lax.div(layer, 2), lax.rem(layer, 2)
    other = 1 - core
    sibling = {"layer": y * 2 + other}
    z_next, z_prev = {"col": lax.rem(z + 1, RING)}, {"col": lax.rem(z + RING - 1, RING)}
    x_next, x_prev = {"row": lax.rem(x + 1, RING)}, {"row": lax.rem(x + RING - 1, RING)}
    way = 1 - 2 * core
    y_long = {"layer": lax.rem(y + way + RING, RING) * 2 + core}
    y_short = {"layer": lax.rem(y - way + RING, RING) * 2 + core}

    barrier = pltpu.get_barrier_semaphore()
    for step in range(1, RING):
        pl.semaphore_signal(barrier, inc=1, device_id={"col": lax.rem(z + step, RING)}, device_id_type=MESH)
        pl.semaphore_signal(barrier, inc=1, device_id={"row": lax.rem(x + step, RING)}, device_id_type=MESH)
    for device in (y_long, y_short, sibling):
        pl.semaphore_signal(barrier, inc=1, device_id=device, device_id_type=MESH)

    own_a = core * 16 + z * 2
    own_b = core * 8 + x
    own = [
        pltpu.make_async_copy(a_in, a_buf.at[pl.ds(own_a, 2)], own_sem.at[0]),
        pltpu.make_async_copy(b_in, b_buf.at[pl.ds(own_b, 1)], own_sem.at[1]),
    ]
    for copy in own:
        copy.start()
    lane = lax.broadcasted_iota(jnp.int32, (1, BS), 1)
    first = jnp.where(lane == core * 64 + a_slot[0], own_a + 1, 0)
    a_tab[z] = jnp.where(lane == core * 64 + a_slot[1], own_a + 2, first)
    b_tab[x] = jnp.where(lane == core * 32 + b_slot[0], own_b + 1, 0)
    a_buf[32] = jnp.zeros((BS, BS), jnp.bfloat16)
    b_buf[16] = jnp.zeros((BS, BS), jnp.bfloat16)
    comp[KEPT] = jnp.zeros((BS, BS), jnp.float32)

    pl.semaphore_wait(barrier, 2 * (RING - 1) + 3)

    def push(src, dst, send, recv, device):
        pltpu.make_async_remote_copy(
            src_ref=src, dst_ref=dst, send_sem=send, recv_sem=recv, device_id=device, device_id_type=MESH
        ).start()

    def push_a(src, origin, first, count, way, hop, device):
        push(src, a_buf.at[pl.ds(core * 16 + origin * 2 + first, count)], a_send, a_recv.at[way, hop], device)

    def push_b(src, origin, first, count, way, hop, device):
        push(src, b_buf.at[core * 8 + origin, pl.ds(first, count)], b_send, b_recv.at[way, hop], device)

    def a_part(origin, first, count):
        return a_buf.at[pl.ds(core * 16 + origin * 2 + first, count)]

    def b_part(origin, first, count):
        return b_buf.at[core * 8 + origin, pl.ds(first, count)]

    push_a(a_in, z, 0, 2, 0, 0, z_next)
    push_a(a_in, z, 0, 2, 1, 0, z_prev)
    push_b(b_in.at[0], x, 0, BS, 0, 0, x_next)
    push_b(b_in.at[0], x, 0, BS, 1, 0, x_prev)
    for step in range(1, RING):
        push(a_tab.at[z], a_tab.at[z], tab_send.at[0], tab_recv.at[0], {"col": lax.rem(z + step, RING)})
        push(b_tab.at[x], b_tab.at[x], tab_send.at[1], tab_recv.at[1], {"row": lax.rem(x + step, RING)})
    push(a_in, a_part(z, 0, 2), a_send, sib_recv.at[0], sibling)
    push(b_in.at[0], b_part(x, 0, BS), b_send, sib_recv.at[1], sibling)

    def pick(t, carry):
        count = jnp.int32(0)
        picks = [jnp.int32(0)] * KEPT
        for j in range(COLS):
            bit = mask[t * 2 + core, j]
            for q in range(KEPT):
                picks[q] = picks[q] + jnp.where(count == q, bit * j, 0)
            count = count + bit
        for q in range(KEPT):
            sel[t, q] = picks[q]
        return carry

    lax.fori_loop(0, RING, pick, 0)

    for hop in range(1, 5):
        a_up, a_down = lax.rem(z + RING - hop, RING), lax.rem(z + hop, RING)
        b_up, b_down = lax.rem(x + RING - hop, RING), lax.rem(x + hop, RING)
        a_whole, b_whole = ((0, 2), (0, BS)) if hop < 4 else ((0, 1), (0, BS // 2))
        a_rest, b_rest = ((0, 2), (0, BS)) if hop < 4 else ((1, 1), (BS // 2, BS // 2))
        a_next = ((0, 2), (0, 2)) if hop < 3 else ((0, 1), (1, 1))
        b_next = ((0, BS), (0, BS)) if hop < 3 else ((0, BS // 2), (BS // 2, BS // 2))
        wait_bytes(a_part(a_up, *a_whole), a_recv.at[0, hop - 1])
        if hop < 4:
            push_a(a_part(a_up, *a_next[0]), a_up, *a_next[0], 0, hop, z_next)
        wait_bytes(a_part(a_down, *a_rest), a_recv.at[1, hop - 1])
        if hop < 4:
            push_a(a_part(a_down, *a_next[1]), a_down, *a_next[1], 1, hop, z_prev)
        push(a_part(a_up, *a_whole), a_part(a_up, *a_whole), a_send, sib_recv.at[0], sibling)
        push(a_part(a_down, *a_rest), a_part(a_down, *a_rest), a_send, sib_recv.at[0], sibling)
        wait_bytes(b_part(b_up, *b_whole), b_recv.at[0, hop - 1])
        if hop < 4:
            push_b(b_part(b_up, *b_next[0]), b_up, *b_next[0], 0, hop, x_next)
        wait_bytes(b_part(b_down, *b_rest), b_recv.at[1, hop - 1])
        if hop < 4:
            push_b(b_part(b_down, *b_next[1]), b_down, *b_next[1], 1, hop, x_prev)
        push(b_part(b_up, *b_whole), b_part(b_up, *b_whole), b_send, sib_recv.at[1], sibling)
        push(b_part(b_down, *b_rest), b_part(b_down, *b_rest), b_send, sib_recv.at[1], sibling)
        if hop == 2:
            wait_bytes(a_tab.at[pl.ds(0, RING - 1)], tab_recv.at[0])
            wait_bytes(b_tab.at[pl.ds(0, RING - 1)], tab_recv.at[1])
            sum_tx[0] = jnp.max(a_tab[...], axis=0)
            sum_tx[1] = jnp.max(b_tab[...], axis=0)
            push(sum_tx, sum_rx, tab_send.at[2], tab_recv.at[2], sibling)
        if hop == 3:
            wait_bytes(sum_rx, tab_recv.at[2])
            both = jnp.maximum(sum_tx[...], sum_rx[...])
            tab_v[0] = jnp.where(both[0] > 0, both[0] - 1, 32)
            tab_v[1] = jnp.where(both[1] > 0, both[1] - 1, 16)
            pltpu.make_async_copy(tab_v, tab_s, tab_local).start()
    pltpu.make_async_copy(tab_v, tab_s, tab_local).wait()
    for copy in own:
        copy.wait()
    wait_bytes(a_buf.at[pl.ds(other * 16, 16)], sib_recv.at[0])
    wait_bytes(b_buf.at[pl.ds(other * 8, 8)], sib_recv.at[1])

    slices = [(s, kk) for s in range(2) for kk in range(INNER)]

    def partial(t):
        row = t * 2 + core
        left = jnp.concatenate([a_buf[tab_s[0, 0, s * 64 + row * INNER + kk]] for s, kk in slices], axis=1)
        sums = []
        for p in range(KEPT // 2):
            right = jnp.concatenate(
                [
                    jnp.concatenate(
                        [b_buf[tab_s[1, 0, s * 32 + kk * COLS + sel[t, 2 * p + q]]] for q in range(2)], axis=1
                    )
                    for s, kk in slices
                ],
                axis=0,
            )
            sums.append(jnp.dot(left, right, preferred_element_type=jnp.float32))
        return sums

    def received(slot, p):
        wait_bytes(rx.at[slot, p], rs_recv.at[slot, p, 0])
        wait_bytes(rx_scale.at[slot, p], rs_recv.at[slot, p, 1])
        return rx[slot, p].astype(jnp.int32).astype(jnp.float32) * rx_scale[slot, p]

    def send(slot, p, value, device):
        top = jnp.maximum(jnp.max(jnp.abs(value), axis=0, keepdims=True), TINY)
        tx_scale[slot, p] = top * (1.0 / TOP)
        tx[slot, p] = jnp.round(value * (TOP / top)).astype(jnp.int32).astype(jnp.int16)
        push(tx_scale.at[slot, p], rx_scale.at[slot, p], rs_send.at[slot, p, 1], rs_recv.at[slot, p, 1], device)
        push(tx.at[slot, p], rx.at[slot, p], rs_send.at[slot, p, 0], rs_recv.at[slot, p, 0], device)

    for hop in range(4):
        t = lax.rem(y + way * (4 - hop) + RING, RING)
        sums = partial(t)
        for p in range(KEPT // 2):
            value = sums[p] if hop == 0 else sums[p] + received(hop - 1, p)
            send(hop, p, value, y_long)
        if hop < 3:
            t = lax.rem(y - way * (3 - hop) + RING, RING)
            sums = partial(t)
            for p in range(KEPT // 2):
                value = sums[p] if hop == 0 else sums[p] + received(3 + hop, p)
                send(4 + hop, p, value, y_short)
    sums = partial(y)
    for p in range(KEPT // 2):
        value = sums[p] + received(6, p) + received(3, p)
        for q in range(2):
            comp[2 * p + q] = value[:, q * BS : (q + 1) * BS]
    count = jnp.int32(0)
    for j in range(COLS):
        bit = mask[layer, j]
        out[:, j * BS : (j + 1) * BS] = comp[jnp.where(bit == 1, count, KEPT)]
        count = count + bit

    wait_bytes(a_buf.at[pl.ds(0, 30)], a_send)
    wait_bytes(b_buf.at[pl.ds(0, 15)], b_send)
    wait_bytes(a_tab.at[pl.ds(0, RING - 1)], tab_send.at[0])
    wait_bytes(b_tab.at[pl.ds(0, RING - 1)], tab_send.at[1])
    wait_bytes(sum_tx, tab_send.at[2])
    for slot in range(7):
        for p in range(KEPT // 2):
            wait_bytes(tx.at[slot, p], rs_send.at[slot, p, 0])
            wait_bytes(tx_scale.at[slot, p], rs_send.at[slot, p, 1])


def on_device(a_blocks, a_slot, b_blocks, b_slot, c_mask):
    vmem, smem, dma = pltpu.VMEM, pltpu.SMEM, pltpu.SemaphoreType.DMA
    any_space = pl.BlockSpec(memory_space=pl.ANY)
    scalars = pl.BlockSpec(memory_space=smem)
    return pl.pallas_call(
        kernel,
        out_shape=jax.ShapeDtypeStruct((BS, COLS * BS), jnp.float32),
        in_specs=[any_space, scalars, any_space, scalars, scalars],
        out_specs=pl.BlockSpec(memory_space=vmem),
        scratch_shapes=[
            vmem((33, BS, BS), jnp.bfloat16),
            vmem((17, BS, BS), jnp.bfloat16),
            vmem((RING, 1, BS), jnp.int32),
            vmem((RING, 1, BS), jnp.int32),
            vmem((2, 1, BS), jnp.int32),
            vmem((2, 1, BS), jnp.int32),
            vmem((2, 1, BS), jnp.int32),
            smem((2, 1, BS), jnp.int32),
            smem((RING, KEPT), jnp.int32),
            vmem((7, 2, BS, 2 * BS), jnp.int16),
            vmem((7, 2, 1, 2 * BS), jnp.float32),
            vmem((7, 2, BS, 2 * BS), jnp.int16),
            vmem((7, 2, 1, 2 * BS), jnp.float32),
            vmem((KEPT + 1, BS, BS), jnp.float32),
            dma((2,)),
            dma((2, 4)),
            dma((2, 4)),
            dma((2,)),
            dma((3,)),
            dma(()),
            dma(()),
            dma(()),
            dma((3,)),
            dma((7, 2, 2)),
            dma((7, 2, 2)),
        ],
        compiler_params=pltpu.CompilerParams(
            collective_id=0, has_side_effects=True, vmem_limit_bytes=40 * 1024 * 1024
        ),
    )(a_blocks, a_slot, b_blocks, b_slot, c_mask)


def solution(mesh):
    in_specs = (
        P(("row", "col", "layer"), None, None),
        P(("row", "col", "layer")),
        P(("row", "col", "layer"), None, None),
        P(("row", "col", "layer")),
        P("row", "col"),
    )
    out_specs = P(("row", "layer"), "col")
    return jax.shard_map(on_device, mesh=mesh, in_specs=in_specs, out_specs=out_specs, check_vma=False)
```

time: 195 us -> 60.8 us (0.31)
  waiting for transfers between devices: 88.2 us -> 0 us
  blocking collectives: 76.6 us -> 0 us
  Pallas kernels: 0 us -> 56.7 us
  between operations: 14.1 us -> 0.67 us
  matrix products: 8.67 us -> 0 us
  other arithmetic: 2.71 us -> 0 us
    reduce_scatter x1 -> x0, waiting for transfers between devices: 88.2 us -> none  [on_device(): lax.psum_scatter(partial_value, 'layer', scatter_dimension=0, tiled=True)]
    all_gather x4 -> x0, blocking collectives: 76.6 us -> none  [the longest x1 33 us: on_device(): lax.all_gather(a_blocks, 'col', axis=0, tiled=True)]
    pallas_call x0 -> x1, Pallas kernels: none -> 56.7 us  [on_device(): pl.pallas_call(kernel, out_shape=jax.ShapeDtypeStruct((BS, COLS * BS), jn...]
    dot_general x4 -> x0, matrix products: 8.67 us -> none  [the longest x1 7.23 us: on_device(): jnp.dot(a_matrix, b_matrix, preferred_element_type=jnp.float32)]
    reshape x1 -> x0, local copies, waits for them, and re-layouts: 2.93 us -> none  [on_device(): a_matrix = a_dense.astype(jnp.bfloat16).reshape(MBP, KBL, width, width).t...]
    mul x1 -> x0, other arithmetic: 1.97 us -> none  [on_device(): summed.reshape(rows_dev, NBP, width) * row_mask[:, :, None]]
  transfers between devices with their start and end apart: 1 -> 0, of which waited for: 1 -> 0; matrix products, arithmetic and copies ran while one was open for 0% -> 0% of each run, Pallas kernels for 0% -> 0%
where the time goes in v1:
time: 60.8 us; the launch traced here: 60.5 us
  Pallas kernels  56.7 us (93%)
  local copies, waits for them, and re-layouts  3.16 us (5%)
  between operations  0.67 us (1%)
    pallas_call x1, Pallas kernels, on_device(): pl.pallas_call(kernel, out_shape=jax.ShapeDtypeStruct((BS, COLS * BS), jn...  56.7 us
    unnamed x8, local copies, waits for them, and re-layouts  3.16 us

profile of v1, /device:TPU:1, one launch (start us, length us, event | category | flops | bytes accessed | tf_op | source)
XLA Modules:
  0.0 60.5 jit_solution(7184626097819399183)
XLA Ops:
  0.7 0.0 copy-start.2
  0.7 0.8 %copy.6.mask = s32[16,8]{1,0:T(8,128)S(1)} copy(s32[16,8]{0,1:T(8,128)} %param.9) | data formatting | bytes 1024 | tf_op args[4]
  1.4 0.0 copy-done.2
  1.4 0.0 copy-start
  1.4 0.8 %copy-done = bf16[2,128,128]{2,1,0:T(8,128)(2,1)S(1)} copy-done((bf16[2,128,128]{2,1,0:T(8,128)(2,1)S(1)}, bf16[2,128,128]{2,1,0:T(8,128)(2,1)}, u32[]{:S(2)}) %copy-start) | copy-done | bytes 65560
  2.3 0.0 copy-start.1
  2.3 0.8 %copy-done.1 = bf16[1,128,128]{2,1,0:T(8,128)(2,1)S(1)} copy-done((bf16[1,128,128]{2,1,0:T(8,128)(2,1)S(1)}, bf16[1,128,128]{2,1,0:T(8,128)(2,1)}, u32[]{:S(2)}) %copy-start.1) | copy-done | bytes 32792
  3.0 56.7 %shard_map.55 = f32[128,1024]{1,0:T(8,128)S(1)} custom-call(bf16[2,128,128]{2,1,0:T(8,128)(2,1)S(1)} %copy-done, s32[2]{0:T(128)S(1)} %copy-done.2, bf16[1,128,128]{2,1,0:T(8,128)(2,1)S(1)} %copy-done.1, s32[1]{0:T(128)S(6)} %copy.8.b_slot, s32[16,8]{1,0:T(8,128)S(1)} %copy.6.mask), custom_call_target="tpu_custom_call" | custom-call | tf_op jit(solution)/shard_map/pallas_call | solution.py:216
  59.8 0.8 %copy.9 = f32[128,1024]{1,0:T(8,128)} copy(f32[128,1024]{1,0:T(8,128)S(1)} %shard_map.55) | data formatting | bytes 1048576
Async XLA Ops:
  0.7 0.8 %copy-start.2 = (s32[2]{0:T(128)S(1)}, s32[2]{0:T(128)}, u32[]{:S(2)}) copy-start(s32[2]{0:T(128)} %a_slot.1) | copy-start | bytes 28
  1.4 0.8 %copy-start = (bf16[2,128,128]{2,1,0:T(8,128)(2,1)S(1)}, bf16[2,128,128]{2,1,0:T(8,128)(2,1)}, u32[]{:S(2)}) copy-start(bf16[2,128,128]{2,1,0:T(8,128)(2,1)} %a_in.1) | copy-start | bytes 196612
  2.3 0.8 %copy-start.1 = (bf16[1,128,128]{2,1,0:T(8,128)(2,1)S(1)}, bf16[1,128,128]{2,1,0:T(8,128)(2,1)}, u32[]{:S(2)}) copy-start(bf16[1,128,128]{2,1,0:T(8,128)(2,1)} %b_in.1) | copy-start | bytes 98308

commit v2 on v1

v2 whole, which is shorter than its diff:
```python
import functools

import jax
import jax.numpy as jnp
from jax import lax
from jax.experimental import pallas as pl
from jax.experimental.pallas import tpu as pltpu
from jax.sharding import PartitionSpec as P

MESH = pl.DeviceIdType.MESH
BS = 128
ROWS = 16
INNER = 4
COLS = 8
KEPT = 4
RING = 8
TOP = 32760.0
TINY = 1e-30


def wait_bytes(ref, sem):
    pltpu.make_async_copy(ref, ref, sem).wait()


def kernel(
    a_in, a_slot_in, b_in, b_slot_in, mask_in, out,
    a_slot, b_slot, mask, a_buf, b_buf, a_tab, b_tab, tab_v, tab_s, sel, tx, tx_scale, rx, rx_scale, comp,
    in_sem, own_sem, z_in, x_in, y_in, sib_in, a_recv, b_recv, sib_recv, tab_recv, tab_local,
    a_send, b_send, tab_send, rs_recv, rs_send,
):
    x, z, layer = lax.axis_index("row"), lax.axis_index("col"), lax.axis_index("layer")
    y, core = lax.div(layer, 2), lax.rem(layer, 2)
    other = 1 - core
    twin = y * 2 + other
    sibling = {"layer": twin}
    y_up, y_down = lax.rem(y + 1, RING), lax.rem(y + RING - 1, RING)
    way = 1 - 2 * core
    y_long = {"layer": lax.rem(y + way + RING, RING) * 2 + core}
    y_short = {"layer": lax.rem(y - way + RING, RING) * 2 + core}

    loads = [
        pltpu.make_async_copy(a_slot_in, a_slot, in_sem.at[0]),
        pltpu.make_async_copy(b_slot_in, b_slot, in_sem.at[1]),
        pltpu.make_async_copy(mask_in, mask, in_sem.at[2]),
    ]
    for copy in loads:
        copy.start()

    barrier = pltpu.get_barrier_semaphore()

    def signal(sem, device):
        pl.semaphore_signal(sem, inc=1, device_id=device, device_id_type=MESH)

    for p in range(1, RING):

        @pl.when(p > z)
        def _():
            signal(barrier, {"col": p})
            signal(barrier, {"col": p, "layer": twin})

        @pl.when(p > x)
        def _():
            signal(barrier, {"row": p})
            signal(barrier, {"row": p, "layer": twin})

    for peer in (y_up, y_down):

        @pl.when(peer > y)
        def _():
            signal(barrier, {"layer": peer * 2 + core})

    @pl.when(core == 0)
    def _():
        signal(barrier, sibling)

    own_a = core * 16 + z * 2
    own_b = core * 8 + x
    own = [
        pltpu.make_async_copy(a_in, a_buf.at[pl.ds(own_a, 2)], own_sem.at[0]),
        pltpu.make_async_copy(b_in, b_buf.at[pl.ds(own_b, 1)], own_sem.at[1]),
    ]
    for copy in own:
        copy.start()
    lower_y = jnp.where(y_up < y, 1, 0) + jnp.where(y_down < y, 1, 0)
    n_lower = 2 * z + 2 * x + lower_y + core

    @pl.when(n_lower > 0)
    def _():
        pl.semaphore_wait(barrier, n_lower)

    def push(src, dst, send, recv, device):
        pltpu.make_async_remote_copy(
            src_ref=src, dst_ref=dst, send_sem=send, recv_sem=recv, device_id=device, device_id_type=MESH
        ).start()

    def push_a(p):
        push(a_in, a_buf.at[pl.ds(own_a, 2)], a_send, a_recv.at[z], {"col": p})

    def push_b(p):
        push(b_in, b_buf.at[pl.ds(own_b, 1)], b_send, b_recv.at[x], {"row": p})

    def push_a_tab(device):
        row = a_tab.at[core * 8 + z]
        push(row, row, tab_send.at[0], tab_recv.at[0], device)

    def push_b_tab(device):
        row = b_tab.at[core * 8 + x]
        push(row, row, tab_send.at[1], tab_recv.at[1], device)

    for p in range(RING - 1):

        @pl.when(p < z)
        def _():
            push_a(p)

    for p in range(RING - 1):

        @pl.when(p < z)
        def _():
            signal(z_in.at[core, z], {"col": p})
            signal(z_in.at[core, z], {"col": p, "layer": twin})

        @pl.when(p < x)
        def _():
            signal(x_in.at[core, x], {"row": p})
            signal(x_in.at[core, x], {"row": p, "layer": twin})

    @pl.when(y_up < y)
    def _():
        signal(y_in.at[1], {"layer": y_up * 2 + core})

    @pl.when(y_down < y)
    def _():
        signal(y_in.at[0], {"layer": y_down * 2 + core})

    @pl.when(core == 1)
    def _():
        signal(sib_in, sibling)

    for copy in loads:
        copy.wait()
    lane = lax.broadcasted_iota(jnp.int32, (1, BS), 1)
    first = jnp.where(lane == core * 64 + a_slot[0], own_a + 1, 0)
    a_tab[core * 8 + z] = jnp.where(lane == core * 64 + a_slot[1], own_a + 2, first)
    b_tab[core * 8 + x] = jnp.where(lane == core * 32 + b_slot[0], own_b + 1, 0)

    for p in range(RING - 1):

        @pl.when(p < z)
        def _():
            push_a_tab({"col": p})
            push_a_tab({"col": p, "layer": twin})

    for p in range(RING - 1):

        @pl.when(p < x)
        def _():
            push_b(p)
            push_b_tab({"row": p})
            push_b_tab({"row": p, "layer": twin})

    @pl.when(core == 0)
    def _():
        pl.semaphore_wait(sib_in, 1)

    push(a_in, a_buf.at[pl.ds(own_a, 2)], a_send, sib_recv.at[0], sibling)
    push(b_in, b_buf.at[pl.ds(own_b, 1)], b_send, sib_recv.at[1], sibling)
    push_a_tab(sibling)
    push_b_tab(sibling)

    a_buf[32] = jnp.zeros((BS, BS), jnp.bfloat16)
    b_buf[16] = jnp.zeros((BS, BS), jnp.bfloat16)
    comp[KEPT] = jnp.zeros((BS, BS), jnp.float32)

    for p in range(1, RING):

        @pl.when(p > x)
        def _():
            pl.semaphore_wait(x_in.at[core, p], 1)
            pl.semaphore_wait(x_in.at[other, p], 1)
            push_b(p)
            push_b_tab({"row": p})
            push_b_tab({"row": p, "layer": twin})

    def pick(t, carry):
        count = jnp.int32(0)
        picks = [jnp.int32(0)] * KEPT
        for j in range(COLS):
            bit = mask[j, t * 2 + core]
            for q in range(KEPT):
                picks[q] = picks[q] + jnp.where(count == q, bit * j, 0)
            count = count + bit
        for q in range(KEPT):
            sel[t, q] = picks[q]
        return carry

    lax.fori_loop(0, RING, pick, 0)

    for p in range(1, RING):

        @pl.when(p > z)
        def _():
            pl.semaphore_wait(z_in.at[core, p], 1)
            pl.semaphore_wait(z_in.at[other, p], 1)
            push_a(p)
            push_a_tab({"col": p})
            push_a_tab({"col": p, "layer": twin})

    @pl.when(y_up > y)
    def _():
        pl.semaphore_wait(y_in.at[0], 1)

    @pl.when(y_down > y)
    def _():
        pl.semaphore_wait(y_in.at[1], 1)

    for p in range(RING):

        @pl.when(p != x)
        def _():
            block = b_buf.at[pl.ds(core * 8 + p, 1)]
            wait_bytes(block, b_recv.at[p])
            push(block, block, b_send, sib_recv.at[1], sibling)

    for p in range(RING):

        @pl.when(p != z)
        def _():
            blocks = a_buf.at[pl.ds(core * 16 + p * 2, 2)]
            wait_bytes(blocks, a_recv.at[p])
            push(blocks, blocks, a_send, sib_recv.at[0], sibling)

    wait_bytes(a_tab.at[pl.ds(0, 15)], tab_recv.at[0])
    wait_bytes(b_tab.at[pl.ds(0, 15)], tab_recv.at[1])
    a_at, b_at = jnp.max(a_tab[...], axis=0), jnp.max(b_tab[...], axis=0)
    tab_v[0] = jnp.where(a_at > 0, a_at - 1, 32)
    tab_v[1] = jnp.where(b_at > 0, b_at - 1, 16)
    to_scalars = pltpu.make_async_copy(tab_v, tab_s, tab_local)
    to_scalars.start()
    for copy in own:
        copy.wait()
    to_scalars.wait()
    wait_bytes(a_buf.at[pl.ds(other * 16, 16)], sib_recv.at[0])
    wait_bytes(b_buf.at[pl.ds(other * 8, 8)], sib_recv.at[1])

    slices = [(s, kk) for s in range(2) for kk in range(INNER)]

    def partial(t):
        row = t * 2 + core
        left = jnp.concatenate([a_buf[tab_s[0, 0, s * 64 + row * INNER + kk]] for s, kk in slices], axis=1)
        sums = []
        for p in range(KEPT // 2):
            right = jnp.concatenate(
                [
                    jnp.concatenate(
                        [b_buf[tab_s[1, 0, s * 32 + kk * COLS + sel[t, 2 * p + q]]] for q in range(2)], axis=1
                    )
                    for s, kk in slices
                ],
                axis=0,
            )
            both = jnp.dot(left, right, preferred_element_type=jnp.float32)
            sums += [both[:, :BS], both[:, BS:]]
        return sums

    def received(slot, q):
        wait_bytes(rx_scale.at[slot, q], rs_recv.at[slot, q, 1])
        wait_bytes(rx.at[slot, q], rs_recv.at[slot, q, 0])
        return rx[slot, q].astype(jnp.int32).astype(jnp.float32) * rx_scale[slot, q]

    def send(slot, q, value, device):
        top = jnp.maximum(jnp.max(jnp.abs(value), axis=0, keepdims=True), TINY)
        tx_scale[slot, q] = top * (1.0 / TOP)
        tx[slot, q] = jnp.round(value * (TOP / top)).astype(jnp.int32).astype(jnp.int16)
        push(tx_scale.at[slot, q], rx_scale.at[slot, q], rs_send.at[slot, q, 1], rs_recv.at[slot, q, 1], device)
        push(tx.at[slot, q], rx.at[slot, q], rs_send.at[slot, q, 0], rs_recv.at[slot, q, 0], device)

    for hop in range(4):
        t = lax.rem(y + way * (4 - hop) + RING, RING)
        sums = partial(t)
        for q in range(KEPT):
            send(hop, q, sums[q] if hop == 0 else sums[q] + received(hop - 1, q), y_long)
        if hop < 3:
            t = lax.rem(y - way * (3 - hop) + RING, RING)
            sums = partial(t)
            for q in range(KEPT):
                send(4 + hop, q, sums[q] if hop == 0 else sums[q] + received(3 + hop, q), y_short)
    sums = partial(y)
    for q in range(KEPT):
        comp[q] = sums[q] + received(6, q) + received(3, q)
    count = jnp.int32(0)
    for j in range(COLS):
        bit = mask[j, layer]
        out[:, j * BS : (j + 1) * BS] = comp[jnp.where(bit == 1, count, KEPT)]
        count = count + bit

    wait_bytes(a_buf.at[pl.ds(0, 30)], a_send)
    wait_bytes(b_buf.at[pl.ds(0, 15)], b_send)
    wait_bytes(a_tab.at[pl.ds(0, 15)], tab_send.at[0])
    wait_bytes(b_tab.at[pl.ds(0, 15)], tab_send.at[1])
    for slot in range(7):
        for q in range(KEPT):
            wait_bytes(tx.at[slot, q], rs_send.at[slot, q, 0])
            wait_bytes(tx_scale.at[slot, q], rs_send.at[slot, q, 1])


def on_device(a_blocks, a_slot, b_blocks, b_slot, c_mask):
    vmem, smem, dma = pltpu.VMEM, pltpu.SMEM, pltpu.SemaphoreType.DMA
    regular = pltpu.SemaphoreType.REGULAR
    return pl.pallas_call(
        kernel,
        out_shape=jax.ShapeDtypeStruct((BS, COLS * BS), jnp.float32),
        in_specs=[pl.BlockSpec(memory_space=pl.ANY)] * 5,
        out_specs=pl.BlockSpec(memory_space=vmem),
        scratch_shapes=[
            smem((2,), jnp.int32),
            smem((1,), jnp.int32),
            smem((COLS, ROWS), jnp.int32),
            vmem((33, BS, BS), jnp.bfloat16),
            vmem((17, BS, BS), jnp.bfloat16),
            vmem((2 * RING, 1, BS), jnp.int32),
            vmem((2 * RING, 1, BS), jnp.int32),
            vmem((2, 1, BS), jnp.int32),
            smem((2, 1, BS), jnp.int32),
            smem((RING, KEPT), jnp.int32),
            vmem((7, KEPT, BS, BS), jnp.int16),
            vmem((7, KEPT, 1, BS), jnp.float32),
            vmem((7, KEPT, BS, BS), jnp.int16),
            vmem((7, KEPT, 1, BS), jnp.float32),
            vmem((KEPT + 1, BS, BS), jnp.float32),
            dma((3,)),
            dma((2,)),
            regular((2, RING)),
            regular((2, RING)),
            regular((2,)),
            regular(()),
            dma((RING,)),
            dma((RING,)),
            dma((2,)),
            dma((2,)),
            dma(()),
            dma(()),
            dma(()),
            dma((2,)),
            dma((7, KEPT, 2)),
            dma((7, KEPT, 2)),
        ],
        compiler_params=pltpu.CompilerParams(
            collective_id=0, has_side_effects=True, vmem_limit_bytes=56 * 1024 * 1024
        ),
    )(a_blocks, a_slot, b_blocks, b_slot, c_mask.T)


def solution(mesh):
    in_specs = (
        P(("row", "col", "layer"), None, None),
        P(("row", "col", "layer")),
        P(("row", "col", "layer"), None, None),
        P(("row", "col", "layer")),
        P("row", "col"),
    )
    out_specs = P(("row", "layer"), "col")
    return jax.shard_map(on_device, mesh=mesh, in_specs=in_specs, out_specs=out_specs, check_vma=False)
```

time: 60.8 us -> 54.1 us (0.89)
  the two profiles are of different devices: /device:TPU:1 before, /device:TPU:14 now
where the time goes in v2:
time: 54.1 us; the launch traced here: 53.9 us
  Pallas kernels  51.3 us (95%)
  local copies, waits for them, and re-layouts  1.89 us (3%)
  between operations  0.66 us (1%)
    pallas_call x1, Pallas kernels, on_device(): pl.pallas_call(kernel, out_shape=jax.ShapeDtypeStruct((BS, COLS * BS), jn...  51.3 us
    unnamed x1, local copies, waits for them, and re-layouts  1.89 us

profile of v2, /device:TPU:14, one launch (start us, length us, event | category | flops | bytes accessed | tf_op | source)
XLA Modules:
  0.0 53.9 jit_solution(2153125311554529371)
XLA Ops:
  0.7 51.3 %shard_map.55 = f32[128,1024]{1,0:T(8,128)} custom-call(bf16[2,128,128]{2,1,0:T(8,128)(2,1)} %a_in.1, s32[2]{0:T(128)} %a_slot_in.1, bf16[1,128,128]{2,1,0:T(8,128)(2,1)} %b_in.1, s32[1]{0:T(128)S(6)} %copy.7.b_slot_in, s32[8,16]{1,0:T(8,128)} %bitcast.1), custom_call_target="tpu_custom_call" | custom-call | tf_op jit(solution)/shard_map/pallas_call | solution.py:310
  52.0 1.9 %copy.8 = f32[128,1024]{1,0:T(8,128)} copy(f32[128,1024]{1,0:T(8,128)} %shard_map.55) | data formatting | bytes 1048576

commit v3 on v2

--- a/solution.py
+++ b/solution.py
@@ -16,6 +16,23 @@
 RING = 8
 TOP = 32760.0
 TINY = 1e-30
+
+
+X_ORDER = Y_ORDER = (0, 1, 2, 3, 7, 6, 5, 4)
+
+
+def place(index, order):
+    found = jnp.int32(0)
+    for n, p in enumerate(order):
+        found = jnp.where(index == p, n, found)
+    return found
+
+
+def member(n, order):
+    found = jnp.int32(0)
+    for m, p in enumerate(order):
+        found = jnp.where(n == m, p, found)
+    return found
 
 
 def wait_bytes(ref, sem):
@@ -48,30 +65,82 @@
 
     barrier = pltpu.get_barrier_semaphore()
 
+    def flag(condition):
+        return jnp.where(condition, 1, 0)
+
     def signal(sem, device):
         pl.semaphore_signal(sem, inc=1, device_id=device, device_id_type=MESH)
 
-    for p in range(1, RING):
-
-        @pl.when(p > z)
-        def _():
-            signal(barrier, {"col": p})
-            signal(barrier, {"col": p, "layer": twin})
-
-        @pl.when(p > x)
-        def _():
-            signal(barrier, {"row": p})
-            signal(barrier, {"row": p, "layer": twin})
-
+    at_x, at_y, at_z, at_core = flag(x == 0), flag(y == 0), flag(z == 0), flag(core == 0)
+    is_zero = at_x * at_y * at_z * at_core
+    x_place, y_place = place(x, X_ORDER), place(y, Y_ORDER)
+    z_rank, x_rank, y_rank = z + 8 * is_zero, x_place + 8 * is_zero, y_place + 8 * is_zero
+    core_rank = core + 2 * is_zero
+    sib_rank = other + 2 * (at_x * at_y * at_z * core)
+
+    def z_peer(p, twin):
+        return p + (8 * (at_x * at_y * (core if twin else at_core)) if p == 0 else 0)
+
+    def x_peer(p, twin):
+        return X_ORDER.index(p) + (8 * (at_y * at_z * (core if twin else at_core)) if p == 0 else 0)
+
+    def y_peer(p):
+        return place(p, Y_ORDER) + 8 * (at_x * at_z * at_core * flag(p == 0))
+
+    def after(peer, me, fn, *args):
+        pl.when(peer > me)(functools.partial(fn, *args))
+
+    def before(peer, me, fn, *args):
+        pl.when(peer < me)(functools.partial(fn, *args))
+
+    def ring(place, own_zero, twin_zero):
+        spot = lax.rem(place - own_zero + RING, RING)
+        turn = twin_zero * flag(place > 0)
+        twin_spot = place - turn
+
+        def over(first, end, shift, fn):
+            def step(n, carry):
+                fn(lax.rem(n + shift, RING))
+                return carry
+
+            lax.fori_loop(first, end, step, 0)
+
+        def all_before(fn):
+            over(0, spot, own_zero, fn)
+
+        def all_after(fn):
+            over(spot + 1, RING, own_zero, fn)
+
+        def twins_before(fn):
+            over(is_zero, twin_spot + 8 * is_zero, turn, fn)
+
+        def twins_after(fn):
+            over(twin_spot + 1 + 8 * is_zero, RING, turn, fn)
+
+        return all_before, all_after, twins_before, twins_after
+
+    z_before, z_later, z_twins_before, z_twins_later = ring(z, at_x * at_y * at_core, at_x * at_y * core)
+    x_before, x_later, x_twins_before, x_twins_later = ring(x_place, at_y * at_z * at_core, at_y * at_z * core)
+
+    def col(p):
+        return {"col": p}
+
+    def col_twin(p):
+        return {"col": p, "layer": twin}
+
+    def row(n):
+        return {"row": member(n, X_ORDER)}
+
+    def row_twin(n):
+        return {"row": member(n, X_ORDER), "layer": twin}
+
+    after(sib_rank, core_rank, signal, barrier, sibling)
     for peer in (y_up, y_down):
-
-        @pl.when(peer > y)
-        def _():
-            signal(barrier, {"layer": peer * 2 + core})
-
-    @pl.when(core == 0)
-    def _():
-        signal(barrier, sibling)
+        after(y_peer(peer), y_rank, signal, barrier, {"layer": peer * 2 + core})
+    x_later(lambda n: signal(barrier, row(n)))
+    x_twins_later(lambda n: signal(barrier, row_twin(n)))
+    z_later(lambda p: signal(barrier, col(p)))
+    z_twins_later(lambda p: signal(barrier, col_twin(p)))
 
     own_a = core * 16 + z * 2
     own_b = core * 8 + x
@@ -81,8 +150,10 @@
     ]
     for copy in own:
         copy.start()
-    lower_y = jnp.where(y_up < y, 1, 0) + jnp.where(y_down < y, 1, 0)
-    n_lower = 2 * z + 2 * x + lower_y + core
+    z_lower = 2 * z - flag(z > 0) * at_x * at_y
+    x_lower = 2 * x_place - flag(x > 0) * at_y * at_z
+    y_lower = flag(y_peer(y_up) < y_rank) + flag(y_peer(y_down) < y_rank)
+    n_lower = jnp.where(is_zero == 1, 4 * (RING - 1), z_lower + x_lower) + y_lower + flag(sib_rank < core_rank)
 
     @pl.when(n_lower > 0)
     def _():
@@ -94,10 +165,10 @@
         ).start()
 
     def push_a(p):
-        push(a_in, a_buf.at[pl.ds(own_a, 2)], a_send, a_recv.at[z], {"col": p})
-
-    def push_b(p):
-        push(b_in, b_buf.at[pl.ds(own_b, 1)], b_send, b_recv.at[x], {"row": p})
+        push(a_in, a_buf.at[pl.ds(own_a, 2)], a_send, a_recv.at[z], col(p))
+
+    def push_b(device):
+        push(b_in, b_buf.at[pl.ds(own_b, 1)], b_send, b_recv.at[x], device)
 
     def push_a_tab(device):
         row = a_tab.at[core * 8 + z]
@@ -107,59 +178,41 @@
         row = b_tab.at[core * 8 + x]
         push(row, row, tab_send.at[1], tab_recv.at[1], device)
 
-    for p in range(RING - 1):
-
-        @pl.when(p < z)
-        def _():
-            push_a(p)
-
-    for p in range(RING - 1):
-
-        @pl.when(p < z)
-        def _():
-            signal(z_in.at[core, z], {"col": p})
-            signal(z_in.at[core, z], {"col": p, "layer": twin})
-
-        @pl.when(p < x)
-        def _():
-            signal(x_in.at[core, x], {"row": p})
-            signal(x_in.at[core, x], {"row": p, "layer": twin})
-
-    @pl.when(y_up < y)
-    def _():
-        signal(y_in.at[1], {"layer": y_up * 2 + core})
-
-    @pl.when(y_down < y)
-    def _():
-        signal(y_in.at[0], {"layer": y_down * 2 + core})
-
-    @pl.when(core == 1)
-    def _():
-        signal(sib_in, sibling)
-
-    for copy in loads:
+    group = lax.div(z, 4)
+    is_end = flag(z == 0) + flag(z == 3) + flag(z == 4) + flag(z == 7)
+    line_of_zero = at_x * at_y * at_core
+    z_inner = {"col": z + 1 - 2 * lax.rem(z, 2)}
+
+    def push_a_if_direct(p):
+        near = flag(lax.div(p, 4) == group)
+        end = flag(p == 0) + flag(p == 3) + flag(p == 4) + flag(p == 7)
+        extra = flag(z == 7) * flag(p == 1)
+        pl.when(near + end + extra > 0)(functools.partial(push_a, p))
+
+    z_before(push_a_if_direct)
+
+    for copy in loads[:2]:
         copy.wait()
     lane = lax.broadcasted_iota(jnp.int32, (1, BS), 1)
     first = jnp.where(lane == core * 64 + a_slot[0], own_a + 1, 0)
     a_tab[core * 8 + z] = jnp.where(lane == core * 64 + a_slot[1], own_a + 2, first)
     b_tab[core * 8 + x] = jnp.where(lane == core * 32 + b_slot[0], own_b + 1, 0)
 
-    for p in range(RING - 1):
-
-        @pl.when(p < z)
-        def _():
-            push_a_tab({"col": p})
-            push_a_tab({"col": p, "layer": twin})
-
-    for p in range(RING - 1):
-
-        @pl.when(p < x)
-        def _():
-            push_b(p)
-            push_b_tab({"row": p})
-            push_b_tab({"row": p, "layer": twin})
-
-    @pl.when(core == 0)
+    z_before(lambda p: push_a_tab(col(p)))
+    z_twins_before(lambda p: push_a_tab(col_twin(p)))
+    z_before(lambda p: signal(z_in.at[core, z], col(p)))
+    z_twins_before(lambda p: signal(z_in.at[core, z], col_twin(p)))
+    x_before(lambda n: push_b(row(n)))
+    x_before(lambda n: push_b_tab(row(n)))
+    x_twins_before(lambda n: push_b_tab(row_twin(n)))
+    x_before(lambda n: signal(x_in.at[core, x], row(n)))
+    x_twins_before(lambda n: signal(x_in.at[core, x], row_twin(n)))
+
+    before(y_peer(y_up), y_rank, signal, y_in.at[1], {"layer": y_up * 2 + core})
+    before(y_peer(y_down), y_rank, signal, y_in.at[0], {"layer": y_down * 2 + core})
+    before(sib_rank, core_rank, signal, sib_in, sibling)
+
+    @pl.when(sib_rank > core_rank)
     def _():
         pl.semaphore_wait(sib_in, 1)
 
@@ -172,15 +225,23 @@
     b_buf[16] = jnp.zeros((BS, BS), jnp.bfloat16)
     comp[KEPT] = jnp.zeros((BS, BS), jnp.float32)
 
-    for p in range(1, RING):
-
-        @pl.when(p > x)
+    def x_after(p):
+        pl.semaphore_wait(x_in.at[core, p], 1)
+        push_b({"row": p})
+        push_b_tab({"row": p})
+
+    def x_after_twin(p):
+        pl.semaphore_wait(x_in.at[other, p], 1)
+        push_b_tab({"row": p, "layer": twin})
+
+    for p in X_ORDER[1:] + (0,):
+
+        @pl.when(p != x)
         def _():
-            pl.semaphore_wait(x_in.at[core, p], 1)
-            pl.semaphore_wait(x_in.at[other, p], 1)
-            push_b(p)
-            push_b_tab({"row": p})
-            push_b_tab({"row": p, "layer": twin})
+            after(x_peer(p, 0), x_rank, x_after, p)
+            after(x_peer(p, 1), x_rank, x_after_twin, p)
+
+    loads[2].wait()
 
     def pick(t, carry):
         count = jnp.int32(0)
@@ -196,40 +257,90 @@
 
     lax.fori_loop(0, RING, pick, 0)
 
-    for p in range(1, RING):
-
-        @pl.when(p > z)
-        def _():
-            pl.semaphore_wait(z_in.at[core, p], 1)
-            pl.semaphore_wait(z_in.at[other, p], 1)
-            push_a(p)
-            push_a_tab({"col": p})
-            push_a_tab({"col": p, "layer": twin})
-
-    @pl.when(y_up > y)
+    def z_after(p):
+        pl.semaphore_wait(z_in.at[core, p], 1)
+        push_a_if_direct(p)
+        push_a_tab({"col": p})
+
+    def z_after_twin(p):
+        pl.semaphore_wait(z_in.at[other, p], 1)
+        push_a_tab({"col": p, "layer": twin})
+
+    def offer(peers):
+        for p in peers:
+
+            @pl.when(p != z)
+            def _():
+                after(z_peer(p, 0), z_rank, z_after, p)
+                after(z_peer(p, 1), z_rank, z_after_twin, p)
+
+    def share_b():
+        for p in range(RING):
+
+            @pl.when(p != x)
+            def _():
+                block = b_buf.at[pl.ds(core * 8 + p, 1)]
+                wait_bytes(block, b_recv.at[p])
+                push(block, block, b_send, sib_recv.at[1], sibling)
+
+    def share_a(peers):
+        for p in peers:
+
+            @pl.when(p != z)
+            def _():
+                blocks = a_buf.at[pl.ds(core * 16 + p * 2, 2)]
+                wait_bytes(blocks, a_recv.at[p])
+
+                inwards = is_end * flag(group != p // 4)
+                if p == 7:
+                    inwards = inwards * flag(z != 0)
+
+                @pl.when(inwards == 1)
+                def _():
+                    push(blocks, blocks, a_send, a_recv.at[p], z_inner)
+
+                push(blocks, blocks, a_send, sib_recv.at[0], sibling)
+
+    forwards = (flag(z == 0) + flag(z == 3)) * (1 - line_of_zero)
+    offer((1, 2, 3))
+
+    @pl.when(group == 0)
+    def _():
+        share_b()
+        share_a((1, 2, 3))
+
+    offer((4, 5))
+
+    @pl.when(forwards == 1)
+    def _():
+        share_a((4,))
+
+    offer((6,))
+
+    @pl.when(forwards == 1)
+    def _():
+        share_a((5,))
+
+    offer((7, 0))
+
+    @pl.when(y_peer(y_up) > y_rank)
     def _():
         pl.semaphore_wait(y_in.at[0], 1)
 
-    @pl.when(y_down > y)
+    @pl.when(y_peer(y_down) > y_rank)
     def _():
         pl.semaphore_wait(y_in.at[1], 1)
 
-    for p in range(RING):
-
-        @pl.when(p != x)
-        def _():
-            block = b_buf.at[pl.ds(core * 8 + p, 1)]
-            wait_bytes(block, b_recv.at[p])
-            push(block, block, b_send, sib_recv.at[1], sibling)
-
-    for p in range(RING):
-
-        @pl.when(p != z)
-        def _():
-            blocks = a_buf.at[pl.ds(core * 16 + p * 2, 2)]
-            wait_bytes(blocks, a_recv.at[p])
-            push(blocks, blocks, a_send, sib_recv.at[0], sibling)
-
+    @pl.when(group == 1)
+    def _():
+        share_b()
+        share_a((1, 2, 3))
+
+    @pl.when(forwards == 0)
+    def _():
+        share_a((4, 5))
+
+    share_a((6, 7, 0))
     wait_bytes(a_tab.at[pl.ds(0, 15)], tab_recv.at[0])
     wait_bytes(b_tab.at[pl.ds(0, 15)], tab_recv.at[1])
     a_at, b_at = jnp.max(a_tab[...], axis=0), jnp.max(b_tab[...], axis=0)
@@ -272,8 +383,8 @@
         top = jnp.maximum(jnp.max(jnp.abs(value), axis=0, keepdims=True), TINY)
         tx_scale[slot, q] = top * (1.0 / TOP)
         tx[slot, q] = jnp.round(value * (TOP / top)).astype(jnp.int32).astype(jnp.int16)
-        push(tx_scale.at[slot, q], rx_scale.at[slot, q], rs_send.at[slot, q, 1], rs_recv.at[slot, q, 1], device)
-        push(tx.at[slot, q], rx.at[slot, q], rs_send.at[slot, q, 0], rs_recv.at[slot, q, 0], device)
+        push(tx_scale.at[slot, q], rx_scale.at[slot, q], rs_send.at[1], rs_recv.at[slot, q, 1], device)
+        push(tx.at[slot, q], rx.at[slot, q], rs_send.at[2 if slot == 0 else 0], rs_recv.at[slot, q, 0], device)
 
     for hop in range(4):
         t = lax.rem(y + way * (4 - hop) + RING, RING)
@@ -294,23 +405,37 @@
         out[:, j * BS : (j + 1) * BS] = comp[jnp.where(bit == 1, count, KEPT)]
         count = count + bit
 
-    wait_bytes(a_buf.at[pl.ds(0, 30)], a_send)
+    wait_bytes(a_buf.at[pl.ds(0, 26)], a_send)
+
+    @pl.when(z == 7)
+    def _():
+        wait_bytes(a_buf.at[pl.ds(0, 2)], a_send)
+
+    @pl.when(is_end == 1)
+    def _():
+        wait_bytes(a_buf.at[pl.ds(0, 6)], a_send)
+
+    @pl.when(is_end * flag(z != 0) == 1)
+    def _():
+        wait_bytes(a_buf.at[pl.ds(0, 2)], a_send)
+
     wait_bytes(b_buf.at[pl.ds(0, 15)], b_send)
     wait_bytes(a_tab.at[pl.ds(0, 15)], tab_send.at[0])
     wait_bytes(b_tab.at[pl.ds(0, 15)], tab_send.at[1])
-    for slot in range(7):
-        for q in range(KEPT):
-            wait_bytes(tx.at[slot, q], rs_send.at[slot, q, 0])
-            wait_bytes(tx_scale.at[slot, q], rs_send.at[slot, q, 1])
+    wait_bytes(tx.at[pl.ds(1, 6)], rs_send.at[0])
+    wait_bytes(tx_scale, rs_send.at[1])
+    wait_bytes(tx.at[0], rs_send.at[2])
 
 
 def on_device(a_blocks, a_slot, b_blocks, b_slot, c_mask):
     vmem, smem, dma = pltpu.VMEM, pltpu.SMEM, pltpu.SemaphoreType.DMA
     regular = pltpu.SemaphoreType.REGULAR
+    operands = (a_blocks, a_slot, b_blocks, b_slot, c_mask.T)
+    operands = [operand if operand is b_slot else pltpu.with_memory_space_constraint(operand, pltpu.HBM) for operand in operands]
     return pl.pallas_call(
         kernel,
         out_shape=jax.ShapeDtypeStruct((BS, COLS * BS), jnp.float32),
-        in_specs=[pl.BlockSpec(memory_space=pl.ANY)] * 5,
+        in_specs=[pl.BlockSpec(memory_space=pltpu.HBM)] * 5,
         out_specs=pl.BlockSpec(memory_space=vmem),
         scratch_shapes=[
             smem((2,), jnp.int32),
@@ -343,12 +468,12 @@
             dma(()),
             dma((2,)),
             dma((7, KEPT, 2)),
-            dma((7, KEPT, 2)),
+            dma((3,)),
         ],
         compiler_params=pltpu.CompilerParams(
-            collective_id=0, has_side_effects=True, vmem_limit_bytes=56 * 1024 * 1024
+            collective_id=0, has_side_effects=True, vmem_limit_bytes=40 * 1024 * 1024
         ),
-    )(a_blocks, a_slot, b_blocks, b_slot, c_mask.T)
+    )(*operands)
 
 
 def solution(mesh):

time: 54.1 us -> 50.7 us (0.937)
  the two profiles are of different devices: /device:TPU:14 before, /device:TPU:128 now
where the time goes in v3:
time: 50.7 us; the launch traced here: 50.5 us
  Pallas kernels  49.1 us (97%)
  local copies, waits for them, and re-layouts  0.8 us (2%)
  between operations  0.66 us (1%)
    pallas_call x1, Pallas kernels, on_device(): pl.pallas_call(kernel, out_shape=jax.ShapeDtypeStruct((BS, COLS * BS), jn...  49.1 us

profile of v3, /device:TPU:128, one launch (start us, length us, event | category | flops | bytes accessed | tf_op | source)
XLA Modules:
  0.0 50.5 jit_solution(10181019557092352431)
XLA Ops:
  0.7 49.1 %shard_map.55 = f32[128,1024]{1,0:T(8,128)S(1)} custom-call(bf16[2,128,128]{2,1,0:T(8,128)(2,1)} %a_in.1, s32[2]{0:T(128)} %a_slot_in.1, bf16[1,128,128]{2,1,0:T(8,128)(2,1)} %b_in.1, s32[1]{0:T(128)S(6)} %copy.7.b_slot_in, s32[8,16]{1,0:T(8,128)} %bitcast.1), custom_call_target="tpu_custom_call" | custom-call | tf_op jit(solution)/shard_map/pallas_call | solution.py:435
  49.7 0.8 %copy.8 = f32[128,1024]{1,0:T(8,128)} copy(f32[128,1024]{1,0:T(8,128)S(1)} %shard_map.55) | data formatting | bytes 1048576

commit v4 on v3

--- a/solution.py
+++ b/solution.py
@@ -18,6 +18,7 @@
 TINY = 1e-30
 
 
+DIRECT_TO_1, DIRECT_TO_2 = (6, 7), ()
 X_ORDER = Y_ORDER = (0, 1, 2, 3, 7, 6, 5, 4)
 
 
@@ -51,10 +52,6 @@
     twin = y * 2 + other
     sibling = {"layer": twin}
     y_up, y_down = lax.rem(y + 1, RING), lax.rem(y + RING - 1, RING)
-    way = 1 - 2 * core
-    y_long = {"layer": lax.rem(y + way + RING, RING) * 2 + core}
-    y_short = {"layer": lax.rem(y - way + RING, RING) * 2 + core}
-
     loads = [
         pltpu.make_async_copy(a_slot_in, a_slot, in_sem.at[0]),
         pltpu.make_async_copy(b_slot_in, b_slot, in_sem.at[1]),
@@ -85,7 +82,7 @@
         return X_ORDER.index(p) + (8 * (at_y * at_z * (core if twin else at_core)) if p == 0 else 0)
 
     def y_peer(p):
-        return place(p, Y_ORDER) + 8 * (at_x * at_z * at_core * flag(p == 0))
+        return place(p, Y_ORDER) + 8 * (at_x * at_z * core * flag(p == 0))
 
     def after(peer, me, fn, *args):
         pl.when(peer > me)(functools.partial(fn, *args))
@@ -136,7 +133,7 @@
 
     after(sib_rank, core_rank, signal, barrier, sibling)
     for peer in (y_up, y_down):
-        after(y_peer(peer), y_rank, signal, barrier, {"layer": peer * 2 + core})
+        after(y_peer(peer), y_rank, signal, barrier, {"layer": peer * 2 + other})
     x_later(lambda n: signal(barrier, row(n)))
     x_twins_later(lambda n: signal(barrier, row_twin(n)))
     z_later(lambda p: signal(barrier, col(p)))
@@ -183,10 +180,13 @@
     line_of_zero = at_x * at_y * at_core
     z_inner = {"col": z + 1 - 2 * lax.rem(z, 2)}
 
+    def any_of(index, planes):
+        return sum((flag(index == p) for p in planes), jnp.int32(0))
+
     def push_a_if_direct(p):
         near = flag(lax.div(p, 4) == group)
         end = flag(p == 0) + flag(p == 3) + flag(p == 4) + flag(p == 7)
-        extra = flag(z == 7) * flag(p == 1)
+        extra = flag(p == 1) * any_of(z, DIRECT_TO_1) + flag(p == 2) * any_of(z, DIRECT_TO_2)
         pl.when(near + end + extra > 0)(functools.partial(push_a, p))
 
     z_before(push_a_if_direct)
@@ -208,8 +208,8 @@
     x_before(lambda n: signal(x_in.at[core, x], row(n)))
     x_twins_before(lambda n: signal(x_in.at[core, x], row_twin(n)))
 
-    before(y_peer(y_up), y_rank, signal, y_in.at[1], {"layer": y_up * 2 + core})
-    before(y_peer(y_down), y_rank, signal, y_in.at[0], {"layer": y_down * 2 + core})
+    before(y_peer(y_up), y_rank, signal, y_in.at[1], {"layer": y_up * 2 + other})
+    before(y_peer(y_down), y_rank, signal, y_in.at[0], {"layer": y_down * 2 + other})
     before(sib_rank, core_rank, signal, sib_in, sibling)
 
     @pl.when(sib_rank > core_rank)
@@ -247,7 +247,7 @@
         count = jnp.int32(0)
         picks = [jnp.int32(0)] * KEPT
         for j in range(COLS):
-            bit = mask[j, t * 2 + core]
+            bit = mask[j, t]
             for q in range(KEPT):
                 picks[q] = picks[q] + jnp.where(count == q, bit * j, 0)
             count = count + bit
@@ -255,7 +255,7 @@
             sel[t, q] = picks[q]
         return carry
 
-    lax.fori_loop(0, RING, pick, 0)
+    lax.fori_loop(0, ROWS, pick, 0)
 
     def z_after(p):
         pl.semaphore_wait(z_in.at[core, p], 1)
@@ -292,8 +292,10 @@
                 wait_bytes(blocks, a_recv.at[p])
 
                 inwards = is_end * flag(group != p // 4)
-                if p == 7:
+                if p in DIRECT_TO_1:
                     inwards = inwards * flag(z != 0)
+                if p in DIRECT_TO_2:
+                    inwards = inwards * flag(z != 3)
 
                 @pl.when(inwards == 1)
                 def _():
@@ -356,15 +358,14 @@
 
     slices = [(s, kk) for s in range(2) for kk in range(INNER)]
 
-    def partial(t):
-        row = t * 2 + core
+    def partial(row):
         left = jnp.concatenate([a_buf[tab_s[0, 0, s * 64 + row * INNER + kk]] for s, kk in slices], axis=1)
         sums = []
         for p in range(KEPT // 2):
             right = jnp.concatenate(
                 [
                     jnp.concatenate(
-                        [b_buf[tab_s[1, 0, s * 32 + kk * COLS + sel[t, 2 * p + q]]] for q in range(2)], axis=1
+                        [b_buf[tab_s[1, 0, s * 32 + kk * COLS + sel[row, 2 * p + q]]] for q in range(2)], axis=1
                     )
                     for s, kk in slices
                 ],
@@ -384,21 +385,30 @@
         tx_scale[slot, q] = top * (1.0 / TOP)
         tx[slot, q] = jnp.round(value * (TOP / top)).astype(jnp.int32).astype(jnp.int16)
         push(tx_scale.at[slot, q], rx_scale.at[slot, q], rs_send.at[1], rs_recv.at[slot, q, 1], device)
-        push(tx.at[slot, q], rx.at[slot, q], rs_send.at[2 if slot == 0 else 0], rs_recv.at[slot, q, 0], device)
-
-    for hop in range(4):
-        t = lax.rem(y + way * (4 - hop) + RING, RING)
-        sums = partial(t)
-        for q in range(KEPT):
-            send(hop, q, sums[q] if hop == 0 else sums[q] + received(hop - 1, q), y_long)
-        if hop < 3:
-            t = lax.rem(y - way * (3 - hop) + RING, RING)
-            sums = partial(t)
-            for q in range(KEPT):
-                send(4 + hop, q, sums[q] if hop == 0 else sums[q] + received(3 + hop, q), y_short)
-    sums = partial(y)
-    for q in range(KEPT):
-        comp[q] = sums[q] + received(6, q) + received(3, q)
+        push(tx.at[slot, q], rx.at[slot, q], rs_send.at[0], rs_recv.at[slot, q, 0], device)
+
+    to_up, to_down = {"layer": y_up * 2 + other}, {"layer": y_down * 2 + other}
+    up_half, down_half = (0, 1), (2, 3)
+    sums = partial(lax.rem(y + 4, RING) * 2 + core)
+    for q in up_half:
+        send(0, q, sums[q], to_up)
+    for q in down_half:
+        send(4, q, sums[q], to_down)
+    for hop in range(1, 4):
+        turned = other if hop % 2 else core
+        up = partial(lax.rem(y + 4 - hop, RING) * 2 + turned)
+        down = partial(lax.rem(y + 4 + hop, RING) * 2 + turned)
+        for q in down_half:
+            send(hop, q, up[q] if hop == 1 else up[q] + received(hop - 1, q), to_up)
+        for q in up_half:
+            send(4 + hop, q, down[q] if hop == 1 else down[q] + received(3 + hop, q), to_down)
+        for q in up_half:
+            send(hop, q, up[q] + received(hop - 1, q), to_up)
+        for q in down_half:
+            send(4 + hop, q, down[q] + received(3 + hop, q), to_down)
+    sums = partial(layer)
+    for q in down_half + up_half:
+        comp[q] = sums[q] + received(3, q) + received(7, q)
     count = jnp.int32(0)
     for j in range(COLS):
         bit = mask[j, layer]
@@ -406,25 +416,25 @@
         count = count + bit
 
     wait_bytes(a_buf.at[pl.ds(0, 26)], a_send)
-
-    @pl.when(z == 7)
-    def _():
-        wait_bytes(a_buf.at[pl.ds(0, 2)], a_send)
-
-    @pl.when(is_end == 1)
-    def _():
-        wait_bytes(a_buf.at[pl.ds(0, 6)], a_send)
-
-    @pl.when(is_end * flag(z != 0) == 1)
-    def _():
-        wait_bytes(a_buf.at[pl.ds(0, 2)], a_send)
+    for plane, more in (
+        (0, 4 - len(DIRECT_TO_1)),
+        (3, 4 - len(DIRECT_TO_2)),
+        (4, 4 + (4 in DIRECT_TO_1) + (4 in DIRECT_TO_2)),
+        (5, (5 in DIRECT_TO_1) + (5 in DIRECT_TO_2)),
+        (6, (6 in DIRECT_TO_1) + (6 in DIRECT_TO_2)),
+        (7, 4 + (7 in DIRECT_TO_1) + (7 in DIRECT_TO_2)),
+    ):
+        if more:
+
+            @pl.when(z == plane)
+            def _():
+                wait_bytes(a_buf.at[pl.ds(0, 2 * more)], a_send)
 
     wait_bytes(b_buf.at[pl.ds(0, 15)], b_send)
     wait_bytes(a_tab.at[pl.ds(0, 15)], tab_send.at[0])
     wait_bytes(b_tab.at[pl.ds(0, 15)], tab_send.at[1])
-    wait_bytes(tx.at[pl.ds(1, 6)], rs_send.at[0])
-    wait_bytes(tx_scale, rs_send.at[1])
-    wait_bytes(tx.at[0], rs_send.at[2])
+    wait_bytes(tx.at[pl.ds(0, 7)], rs_send.at[0])
+    wait_bytes(tx_scale.at[pl.ds(0, 7)], rs_send.at[1])
 
 
 def on_device(a_blocks, a_slot, b_blocks, b_slot, c_mask):
@@ -447,11 +457,11 @@
             vmem((2 * RING, 1, BS), jnp.int32),
             vmem((2, 1, BS), jnp.int32),
             smem((2, 1, BS), jnp.int32),
-            smem((RING, KEPT), jnp.int32),
-            vmem((7, KEPT, BS, BS), jnp.int16),
-            vmem((7, KEPT, 1, BS), jnp.float32),
-            vmem((7, KEPT, BS, BS), jnp.int16),
-            vmem((7, KEPT, 1, BS), jnp.float32),
+            smem((ROWS, KEPT), jnp.int32),
+            vmem((8, KEPT, BS, BS), jnp.int16),
+            vmem((8, KEPT, 1, BS), jnp.float32),
+            vmem((8, KEPT, BS, BS), jnp.int16),
+            vmem((8, KEPT, 1, BS), jnp.float32),
             vmem((KEPT + 1, BS, BS), jnp.float32),
             dma((3,)),
             dma((2,)),
@@ -467,8 +477,8 @@
             dma(()),
             dma(()),
             dma((2,)),
-            dma((7, KEPT, 2)),
-            dma((3,)),
+            dma((8, KEPT, 2)),
+            dma((2,)),
         ],
         compiler_params=pltpu.CompilerParams(
             collective_id=0, has_side_effects=True, vmem_limit_bytes=40 * 1024 * 1024

time: 50.7 us -> 49.5 us (0.976)
  the two profiles are of different devices: /device:TPU:128 before, /device:TPU:1 now
where the time goes in v4:
time: 49.5 us; the launch traced here: 49.3 us
  Pallas kernels  47.9 us (97%)
  local copies, waits for them, and re-layouts  0.8 us (2%)
  between operations  0.66 us (1%)
    pallas_call x1, Pallas kernels, on_device(): pl.pallas_call(kernel, out_shape=jax.ShapeDtypeStruct((BS, COLS * BS), jn...  47.9 us

profile of v4, /device:TPU:1, one launch (start us, length us, event | category | flops | bytes accessed | tf_op | source)
XLA Modules:
  0.0 49.3 jit_solution(1627814469642469026)
XLA Ops:
  0.7 47.9 %shard_map.55 = f32[128,1024]{1,0:T(8,128)S(1)} custom-call(bf16[2,128,128]{2,1,0:T(8,128)(2,1)} %a_in.1, s32[2]{0:T(128)} %a_slot_in.1, bf16[1,128,128]{2,1,0:T(8,128)(2,1)} %b_in.1, s32[1]{0:T(128)S(6)} %copy.7.b_slot_in, s32[8,16]{1,0:T(8,128)} %bitcast.1), custom_call_target="tpu_custom_call" | custom-call | tf_op jit(solution)/shard_map/pallas_call | solution.py:445
  48.5 0.8 %copy.8 = f32[128,1024]{1,0:T(8,128)} copy(f32[128,1024]{1,0:T(8,128)S(1)} %shard_map.55) | data formatting | bytes 1048576

commit v5 on v4

--- a/solution.py
+++ b/solution.py
@@ -189,6 +189,19 @@
         extra = flag(p == 1) * any_of(z, DIRECT_TO_1) + flag(p == 2) * any_of(z, DIRECT_TO_2)
         pl.when(near + end + extra > 0)(functools.partial(push_a, p))
 
+    def announce_z():
+        z_before(lambda p: signal(z_in.at[core, z], col(p)))
+        z_twins_before(lambda p: signal(z_in.at[core, z], col_twin(p)))
+
+    def announce_x():
+        x_before(lambda n: signal(x_in.at[core, x], row(n)))
+        x_twins_before(lambda n: signal(x_in.at[core, x], row_twin(n)))
+
+    @pl.when(is_zero == 1)
+    def _():
+        announce_z()
+        announce_x()
+
     z_before(push_a_if_direct)
 
     for copy in loads[:2]:
@@ -200,13 +213,11 @@
 
     z_before(lambda p: push_a_tab(col(p)))
     z_twins_before(lambda p: push_a_tab(col_twin(p)))
-    z_before(lambda p: signal(z_in.at[core, z], col(p)))
-    z_twins_before(lambda p: signal(z_in.at[core, z], col_twin(p)))
+    pl.when(is_zero == 0)(announce_z)
     x_before(lambda n: push_b(row(n)))
     x_before(lambda n: push_b_tab(row(n)))
     x_twins_before(lambda n: push_b_tab(row_twin(n)))
-    x_before(lambda n: signal(x_in.at[core, x], row(n)))
-    x_twins_before(lambda n: signal(x_in.at[core, x], row_twin(n)))
+    pl.when(is_zero == 0)(announce_x)
 
     before(y_peer(y_up), y_rank, signal, y_in.at[1], {"layer": y_up * 2 + other})
     before(y_peer(y_down), y_rank, signal, y_in.at[0], {"layer": y_down * 2 + other})

time: 49.5 us -> 49.5 us (level)
  no operation moved by 1% of the time
where the time goes in v5:
time: 49.5 us; the launch traced here: 49.3 us
  Pallas kernels  47.9 us (97%)
  local copies, waits for them, and re-layouts  0.8 us (2%)
  between operations  0.66 us (1%)
    pallas_call x1, Pallas kernels, on_device(): pl.pallas_call(kernel, out_shape=jax.ShapeDtypeStruct((BS, COLS * BS), jn...  47.9 us

profile of v5, /device:TPU:1, one launch (start us, length us, event | category | flops | bytes accessed | tf_op | source)
XLA Modules:
  0.0 49.3 jit_solution(5404868858976941281)
XLA Ops:
  0.7 47.9 %shard_map.55 = f32[128,1024]{1,0:T(8,128)S(1)} custom-call(bf16[2,128,128]{2,1,0:T(8,128)(2,1)} %a_in.1, s32[2]{0:T(128)} %a_slot_in.1, bf16[1,128,128]{2,1,0:T(8,128)(2,1)} %b_in.1, s32[1]{0:T(128)S(6)} %copy.7.b_slot_in, s32[8,16]{1,0:T(8,128)} %bitcast.1), custom_call_target="tpu_custom_call" | custom-call | tf_op jit(solution)/shard_map/pallas_call | solution.py:456
  48.5 0.8 %copy.8 = f32[128,1024]{1,0:T(8,128)} copy(f32[128,1024]{1,0:T(8,128)S(1)} %shard_map.55) | data formatting | bytes 1048576

commit v6 on v4

--- a/solution.py
+++ b/solution.py
@@ -162,7 +162,7 @@
         ).start()
 
     def push_a(p):
-        push(a_in, a_buf.at[pl.ds(own_a, 2)], a_send, a_recv.at[z], col(p))
+        push(a_in, a_buf.at[pl.ds(own_a, 2)], a_send, a_recv.at[z], col_twin(p))
 
     def push_b(device):
         push(b_in, b_buf.at[pl.ds(own_b, 1)], b_send, b_recv.at[x], device)
@@ -177,8 +177,8 @@
 
     group = lax.div(z, 4)
     is_end = flag(z == 0) + flag(z == 3) + flag(z == 4) + flag(z == 7)
-    line_of_zero = at_x * at_y * at_core
-    z_inner = {"col": z + 1 - 2 * lax.rem(z, 2)}
+    line_of_zero = at_x * at_y * core
+    z_inner = {"col": z + 1 - 2 * lax.rem(z, 2), "layer": twin}
 
     def any_of(index, planes):
         return sum((flag(index == p) for p in planes), jnp.int32(0))
@@ -189,7 +189,7 @@
         extra = flag(p == 1) * any_of(z, DIRECT_TO_1) + flag(p == 2) * any_of(z, DIRECT_TO_2)
         pl.when(near + end + extra > 0)(functools.partial(push_a, p))
 
-    z_before(push_a_if_direct)
+    z_twins_before(push_a_if_direct)
 
     for copy in loads[:2]:
         copy.wait()
@@ -259,11 +259,11 @@
 
     def z_after(p):
         pl.semaphore_wait(z_in.at[core, p], 1)
-        push_a_if_direct(p)
         push_a_tab({"col": p})
 
     def z_after_twin(p):
         pl.semaphore_wait(z_in.at[other, p], 1)
+        push_a_if_direct(p)
         push_a_tab({"col": p, "layer": twin})
 
     def offer(peers):
@@ -288,10 +288,13 @@
 
             @pl.when(p != z)
             def _():
-                blocks = a_buf.at[pl.ds(core * 16 + p * 2, 2)]
+                far = flag(group != p // 4)
+                extra = flag(z == 1) * (p in DIRECT_TO_1) + flag(z == 2) * (p in DIRECT_TO_2)
+                forwarded = far * (1 - is_end) * (1 - extra)
+                blocks = a_buf.at[pl.ds((forwarded * core + (1 - forwarded) * other) * 16 + p * 2, 2)]
                 wait_bytes(blocks, a_recv.at[p])
 
-                inwards = is_end * flag(group != p // 4)
+                inwards = is_end * far
                 if p in DIRECT_TO_1:
                     inwards = inwards * flag(z != 0)
                 if p in DIRECT_TO_2:

time: 49.5 us -> 49.5 us (level)
  no operation moved by 1% of the time
where the time goes in v6:
time: 49.5 us; the launch traced here: 49.3 us
  Pallas kernels  47.9 us (97%)
  local copies, waits for them, and re-layouts  0.8 us (2%)
  between operations  0.66 us (1%)
    pallas_call x1, Pallas kernels, on_device(): pl.pallas_call(kernel, out_shape=jax.ShapeDtypeStruct((BS, COLS * BS), jn...  47.9 us

profile of v6, /device:TPU:1, one launch (start us, length us, event | category | flops | bytes accessed | tf_op | source)
XLA Modules:
  0.0 49.3 jit_solution(15732876019827656989)
XLA Ops:
  0.7 47.9 %shard_map.55 = f32[128,1024]{1,0:T(8,128)S(1)} custom-call(bf16[2,128,128]{2,1,0:T(8,128)(2,1)} %a_in.1, s32[2]{0:T(128)} %a_slot_in.1, bf16[1,128,128]{2,1,0:T(8,128)(2,1)} %b_in.1, s32[1]{0:T(128)S(6)} %copy.7.b_slot_in, s32[8,16]{1,0:T(8,128)} %bitcast.1), custom_call_target="tpu_custom_call" | custom-call | tf_op jit(solution)/shard_map/pallas_call | solution.py:448
  48.5 0.8 %copy.8 = f32[128,1024]{1,0:T(8,128)} copy(f32[128,1024]{1,0:T(8,128)S(1)} %shard_map.55) | data formatting | bytes 1048576
